TPU v7x, 768 devices: a whole 4x8x12 slice. The times are simulated.
768 devices in a mesh: dp: 24 (over x, z_lo), expert: 32 (over z_hi, y, core).
Axes of the slice: x: 4, y: 8, z: 12 (z_hi: 2, z_lo: 6; z = z_hi * 6 + z_lo), core: 2. Of those that a mesh axis runs over, the one named last changes fastest.
Arguments:
- tokens: bfloat16 [6144, 3072], P(('dp', 'expert')), may hold values from -24 to 24
- row_gate: bfloat16 [6144], P(('dp', 'expert')), may hold values from 0.19921875 to 1
- block_mask: int32 [48], P('dp'), may hold values 0 or 1
- weights: bfloat16 [3, 5376, 3072], P(None, 'expert'), may hold values from -0.109375 to 0.109375
- out_grad: bfloat16 [6144, 3072], P(('dp', 'expert')), may hold values from -24 to 24
Outputs:
- mixed: bfloat16 [6144, 3072], P(('dp', 'expert'))
- token_grad: bfloat16 [6144, 3072], P(('dp', 'expert'))
- weight_grad: bfloat16 [3, 5376, 3072], P(None, 'expert', 'dp')
All inputs are finite; a program needn't handle non-finite values. No bound on the sum of `block_mask` on one device may be relied on, other than what follows from the above.
Results may differ from a plain program's by a relative error of at most 0.025.
Values may be sent and summed in bfloat16 or wider, within the bound.
A program may use at most 64 MiB of HBM per device.

v0:
```python
import jax
import jax.numpy as jnp
from jax import lax
from jax.sharding import PartitionSpec as P


def body(tokens, row_gate, block_mask, weights, out_grad):
    hidden_width = weights.shape[1]
    model_width = weights.shape[2]
    combine = row_gate.astype(jnp.float32)
    rows_grad = (combine[:, None] * out_grad.astype(jnp.float32)).astype(jnp.bfloat16)
    gathered, grads_all = (
        lax.all_gather(tokens, "expert", axis=0, tiled=True),
        lax.all_gather(rows_grad, "expert", axis=0, tiled=True),
    )
    row_count = gathered.shape[0]
    block_count = block_mask.shape[0]
    block_rows = row_count // block_count
    row_live = jnp.broadcast_to(
        block_mask.astype(jnp.float32)[:, None], (block_count, block_rows)
    ).reshape(row_count)[:, None]
    pair_weight = weights[:2].reshape(2 * hidden_width, model_width)
    w_down = weights[2]
    pre_act = jnp.einsum(
        "td,fd->tf", (gathered,)[0], pair_weight, preferred_element_type=jnp.float32
    )
    pre_gate = pre_act[:, :hidden_width]
    pre_up = pre_act[:, hidden_width:]
    sigmoid_gate = jax.nn.sigmoid(pre_gate)
    silu_gate = pre_gate * sigmoid_gate
    hidden = (row_live * silu_gate * pre_up).astype(jnp.bfloat16)
    out_term = jnp.dot((hidden,)[0], w_down, preferred_element_type=jnp.float32)
    back_hidden = jnp.einsum(
        "td,fd->tf", (grads_all,)[0], w_down, preferred_element_type=jnp.float32
    )
    slope = sigmoid_gate * (1.0 + pre_gate * (1.0 - sigmoid_gate))
    gate_grad = (row_live * back_hidden * pre_up * slope).astype(jnp.bfloat16)
    up_grad = (row_live * back_hidden * silu_gate).astype(jnp.bfloat16)
    joined = jnp.concatenate([gate_grad, up_grad], axis=1)
    in_term = jnp.dot((joined,)[0], pair_weight, preferred_element_type=jnp.float32)
    down_grad = jnp.einsum("tf,td->fd", hidden, grads_all, preferred_element_type=jnp.float32)
    pair_grad = jnp.einsum(
        "tf,td->fd", joined, gathered, preferred_element_type=jnp.float32
    ).reshape(2, hidden_width, model_width)
    stacked = jnp.concatenate([pair_grad, down_grad[None]], axis=0)
    weight_grad = lax.psum_scatter(
        stacked.astype(jnp.bfloat16), "dp", scatter_dimension=2, tiled=True
    )
    out_sum = lax.psum_scatter(
        out_term.astype(jnp.bfloat16), "expert", scatter_dimension=0, tiled=True
    ).astype(jnp.float32)
    in_sum = lax.psum_scatter(
        in_term.astype(jnp.bfloat16), "expert", scatter_dimension=0, tiled=True
    )
    mixed = (combine[:, None] * out_sum).astype(jnp.bfloat16)
    return (mixed, in_sum, weight_grad)


def solution(mesh):
    in_specs = (
        P(("dp", "expert"), None),
        P(("dp", "expert")),
        P("dp"),
        P(None, "expert", None),
        P(("dp", "expert"), None),
    )
    out_specs = (P(("dp", "expert"), None), P(("dp", "expert"), None), P(None, "expert", "dp"))
    return jax.shard_map(body, mesh=mesh, in_specs=in_specs, out_specs=out_specs, check_vma=False)
```

profile of v0, /device:TPU:1, one launch (start us, length us, event | category | flops | bytes accessed | tf_op | source)
XLA Modules:
  0.0 688.6 jit_solution(14436722861792450386)
XLA Ops:
  7.2 0.7 all-gather.3.cloned.1.call-update
  7.9 0.7 convert_element_type.34
  8.6 1.5 multiply_convert_fusion.3
  10.2 0.7 convert_element_type.35
  10.8 1.7 slice.12
  12.5 0.1 broadcast_bitcast_fusion
  12.6 111.0 %all-gather.3.cloned.1.call-done = bf16[256,3072]{1,0:T(8,128)(2,1)} async-done(((bf16[8,3072]{1,0:T(8,128)(2,1)}), bf16[256,3072]{1,0:T(8,128)(2,1)}) %all-gather.3.cloned.1.call-update) | async-done | bytes 1572880 | tf_op jit(solution)/shard_map/all_gather | solution.py:13
  123.6 2.1 fusion.8
  125.8 97.2 %all-gather.5.cloned.1.call-done = bf16[256,3072]{1,0:T(8,128)(2,1)} async-done(((bf16[8,3072]{1,0:T(8,128)(2,1)}), bf16[256,3072]{1,0:T(8,128)(2,1)}) %all-gather.5.cloned.1.call-update) | async-done | bytes 1572880 | tf_op jit(solution)/shard_map/all_gather | solution.py:14
  223.0 2.4 multiply_convert_fusion.1
  225.4 3.0 convolution_convert_fusion.1
  228.4 0.0 reduce-scatter.10.cloned.1.call-start
  228.4 2.0 fusion
  230.4 0.7 convolution_convert_fusion
  231.1 1.9 pad_maximum_fusion
  233.1 9.9 %copy.8 = bf16[3,168,3072]{1,0,2:T(4,128)(2,1)} copy(bf16[3,168,3072]{2,1,0:T(8,128)(2,1)} %pad_maximum_fusion) | data formatting | bytes 6193152
  242.9 12.4 %reshape.18 = bf16[3072,504]{1,0:T(8,128)(2,1)} reshape(bf16[3072,3,168]{2,1,0:T(4,128)(2,1)} %bitcast.23) | data formatting | bytes 6193152
  255.4 2.2 convolution_convert_fusion.2
  257.6 105.2 %reduce-scatter.6.cloned.1.call-done = bf16[8,3072]{1,0:T(8,128)(2,1)} async-done(((bf16[256,3072]{1,0:T(8,128)(2,1)}), bf16[8,3072]{1,0:T(8,128)(2,1)}) %reduce-scatter.6.cloned.1.call-update) | async-done | bytes 49168 | tf_op jit(solution)/shard_map/reduce_scatter | solution.py:49
  362.8 1.5 multiply_convert_fusion.4
  364.3 155.7 %reduce-scatter.10.cloned.1.call-done = bf16[128,504]{1,0:T(8,128)(2,1)} async-done(((bf16[3072,504]{1,0:T(8,128)(2,1)}), bf16[128,504]{1,0:T(8,128)(2,1)}) %reduce-scatter.10.cloned.1.call-update) | async-done | bytes 129040
  520.0 1.1 reshape.19
  521.0 0.8 copy.9
  521.9 160.2 %reduce-scatter.8.cloned.1.call-done = bf16[8,3072]{1,0:T(8,128)(2,1)} async-done(((bf16[256,3072]{1,0:T(8,128)(2,1)}), bf16[8,3072]{1,0:T(8,128)(2,1)}) %reduce-scatter.8.cloned.1.call-update) | async-done | bytes 49168 | tf_op jit(solution)/shard_map/reduce_scatter | solution.py:52
  (10 shorter events, 0.2 us)
Async XLA Ops:
  7.2 116.5 %all-gather.3.cloned.1.call-start = ((), (), s32[]{:S(2)}) async-start(), calls=%async_computation.3 | async-start | bytes 1622016 | tf_op jit(solution)/shard_map/all_gather | solution.py:13
  7.9 215.1 %all-gather.5.cloned.1.call-start = ((), (), s32[]{:S(2)}) async-start(), calls=%async_computation.5 | async-start | bytes 1622016 | tf_op jit(solution)/shard_map/all_gather | solution.py:14
  10.1 352.7 %reduce-scatter.6.cloned.1.call-start = ((), (), s32[]{:S(2)}) async-start(), calls=%async_computation.4 | async-start | bytes 1622016 | tf_op jit(solution)/shard_map/reduce_scatter | solution.py:49
  228.4 291.6 %reduce-scatter.10.cloned.1.call-start = ((), (), s32[]{:S(2)}) async-start(), calls=%async_computation.7 | async-start | bytes 3276800
  228.4 2.0 copy-start
  255.3 426.7 %reduce-scatter.8.cloned.1.call-start = ((), (), s32[]{:S(2)}) async-start(), calls=%async_computation.6 | async-start | bytes 1622016 | tf_op jit(solution)/shard_map/reduce_scatter | solution.py:52
Sparse Core Ops, SparseCore 0:
  11.9 111.6 all-gather.2
  128.1 94.8 all-gather.4
  228.5 134.2 reduce-scatter.5
  366.1 153.8 reduce-scatter.9
  526.5 155.5 reduce-scatter.7
where the time goes:
time: 693 us; the launch traced here: 689 us
  waiting for transfers between devices  630 us (91%)
  local copies, waits for them, and re-layouts  25.9 us (4%)
  between operations  13.8 us (2%)
  matrix products  12.3 us (2%)
    reduce_scatter x1, waiting for transfers between devices, body(): lax.psum_scatter(in_term.astype(jnp.bfloat16), 'expert', scatter_dimensio...  160 us
    unnamed x6, waiting for transfers between devices  156 us
    all_gather x1, waiting for transfers between devices, body(): lax.all_gather(tokens, 'expert', axis=0, tiled=True)  111 us
    reduce_scatter x1, waiting for transfers between devices, body(): lax.psum_scatter(out_term.astype(jnp.bfloat16), 'expert', scatter_dimensi...  105 us
    all_gather x1, waiting for transfers between devices, body(): lax.all_gather(rows_grad, 'expert', axis=0, tiled=True)  97.2 us
    unnamed x6, local copies, waits for them, and re-layouts  24.2 us
  transfers between devices with their start and end apart: 5, of which 5 were waited for; matrix products, arithmetic and copies ran while one was open for 6% of the time, Pallas kernels for 0%

commit v1 on v0

v1 whole, which is shorter than its diff:
```python
import functools

import jax
import jax.numpy as jnp
from jax import lax
from jax.experimental import pallas as pl
from jax.experimental.pallas import tpu as pltpu
from jax.sharding import PartitionSpec as P

MESH = pl.DeviceIdType.MESH
F32 = jnp.float32
BF16 = jnp.bfloat16

SIZES = (4, 6, 8)
HOP = 2


def kernel(
    sizes, tok_ref, og_ref, gate_ref, mask_ref, w_hbm, mixed_ref, tgrad_ref, wgrad_ref,
    xs, xr, G, TR, W, HT, HR, TERM, SIB, SB, RB, ZS, ZR, DW, SZ, RZ,
    w_sem, xs_s, xs_r, az_s, az_r, ag_s, ag_r, sib_s, sib_r, t_s, t_r, tf_s, tf_r,
    h_s, h_r, ts_s, ts_r, rs_s, rs_r, rz_s, rz_r, fs_s, fs_r, z_s, z_r,
):
    NX, NZ, NY = sizes
    NK = NY // 2
    D = tok_ref.shape[1]
    F = W.shape[1]
    FP = HT.shape[1] // 3
    T = G.shape[1]
    HALF = D // 2
    XC = D // NX
    ZROWS = NY * 16

    dp = lax.axis_index("dp")
    ex = lax.axis_index("expert")
    x, q = dp // NZ, dp % NZ
    zh, y, c = ex // (2 * NY), (ex // 2) % NY, ex % 2
    oc, oz = 1 - c, 1 - zh
    zhp = (zh, oz)

    def at(x=x, q=q, zh=zh, y=y, c=c):
        return (x * NZ + q, zh * (2 * NY) + y * 2 + c)

    def remote(src, dst, ss, rs, to):
        return pltpu.make_async_remote_copy(
            src_ref=src, dst_ref=dst, send_sem=ss, recv_sem=rs, device_id=to, device_id_type=MESH
        )

    sibling = at(c=oc)
    zpartner = at(zh=oz)
    ynext = (at(y=(y + 1) % NY), at(y=(y + NY - 1) % NY))
    xnext = [at(x=(x + r) % NX) for r in range(1, NX)]
    znext = (at(q=(q + 1) % NZ), at(q=(q + NZ - 1) % NZ))

    w_copy = pltpu.make_async_copy(w_hbm, W, w_sem)
    w_copy.start()

    barrier = pltpu.get_barrier_semaphore()
    partners = [sibling, zpartner, *ynext, *xnext, *znext]
    for p in partners:
        pl.semaphore_signal(barrier, inc=1, device_id=p, device_id_type=MESH)

    tok = tok_ref[...].astype(F32)
    combine = gate_ref[:, 0:1]
    rg = (combine * og_ref[...].astype(F32)).astype(BF16).astype(F32)
    xs[...] = jnp.where(c == 0, rg, tok)
    pl.semaphore_wait(barrier, len(partners))

    swap = remote(xs, xr, xs_s, xs_r, sibling)
    swap.start()
    swap.wait()
    got = xr[...]
    own = jnp.where(c == 0, tok, rg)
    block = jnp.concatenate([jnp.where(c == 0, own, got), jnp.where(c == 0, got, own)], axis=0)

    def rows_of(zhv, yv, n=16):
        return pl.ds(pl.multiple_of((zhv * NY + yv) * 16, 16), n)

    def half_of(h):
        return pl.ds(h * HALF, HALF)

    my_rows = rows_of(zh, y)
    G[c, my_rows, :] = block.astype(BF16)

    def sgn(dr):
        return 1 if dr == 0 else -1

    def ag_copy(ph, dr, k, h, origin):
        ref = G.at[c, rows_of(zhp[ph], origin), half_of(h)]
        return remote(ref, ref, ag_s.at[ph, dr, k - 1, h], ag_r.at[ph, dr, k - 1, h], ynext[dr])

    started = []

    def ag_send(ph, dr, k, h):
        cp = ag_copy(ph, dr, k, h, (y + 2 * NY - sgn(dr) * (k - 1)) % NY)
        cp.start()
        started.append(cp)

    def spread(ph, origin):
        rows = rows_of(zhp[ph], origin)
        ref = G.at[c, rows, :]
        remote(ref, ref, sib_s.at[ph], sib_r.at[ph], sibling).start()
        for r in range(1, NX):
            cols = pl.ds(pl.multiple_of(((x + r) % NX) * XC, 128), XC)
            remote(
                G.at[c, rows, cols], TR.at[c, r - 1, rows, :],
                t_s.at[r - 1, ph], t_r.at[r - 1, ph], xnext[r - 1],
            ).start()

    def ag_has(dr, k, h):
        return k < NK or h == dr

    def ag_first(ph):
        for h in range(2):
            for dr in range(2):
                if ag_has(dr, 1, h):
                    ag_send(ph, dr, 1, h)
        spread(ph, y)

    def ag_step(ph, k):
        for h in range(2):
            for dr in range(2):
                if not ag_has(dr, k, h):
                    continue
                origin = (y + 2 * NY - sgn(dr) * k) % NY
                ag_copy(ph, dr, k, h, origin).wait_recv()
                if k < NK and ag_has(dr, k + 1, h):
                    ag_send(ph, dr, k + 1, h)
        spread(ph, (y + NY - k) % NY)
        if k < NK:
            spread(ph, (y + k) % NY)

    az = remote(G.at[c, my_rows, :], G.at[c, my_rows, :], az_s, az_r, zpartner)
    az.start()
    ag_first(0)
    order = [(0, k) for k in range(1, NK // 2 + 1)] + [(1, 0)]
    late0 = [(0, k) for k in range(NK // 2 + 1, NK + 1)]
    late1 = [(1, k) for k in range(1, NK + 1)]
    while late0 or late1:
        if late0:
            order.append(late0.pop(0))
        if late1:
            order.append(late1.pop(0))
    for ph, k in order:
        if k == 0:
            there = G.at[c, rows_of(oz, y), :]
            remote(there, there, az_s, az_r, zpartner).wait_recv()
            ag_first(1)
        else:
            ag_step(ph, k)
    w_copy.wait()
    for ph in range(2):
        ref = G.at[oc, rows_of(zhp[ph], 0, ZROWS), :]
        remote(ref, ref, sib_s.at[ph], sib_r.at[ph], sibling).wait_recv()

    def contract(m, a):
        def step(i, acc):
            cols = pl.ds(pl.multiple_of(i * XC, 128), XC)
            return acc + lax.dot_general(
                W[m, :, cols], G[a, :, cols], (((1,), (1,)), ((), ())), preferred_element_type=F32
            )
        return lax.fori_loop(0, NX, step, jnp.zeros((F, T), F32))

    pre_gate, pre_up, back = contract(0, 0), contract(1, 0), contract(2, 1)
    lane = lax.broadcasted_iota(jnp.int32, (1, T), 1)
    live = jnp.where(lane < T // 2, mask_ref[0], mask_ref[1]).astype(F32)
    sig = jax.nn.sigmoid(pre_gate)
    silu = pre_gate * sig
    hidden = live * silu * pre_up
    gate_grad = live * back * pre_up * (sig * (1.0 + pre_gate * (1.0 - sig)))
    up_grad = live * back * silu
    pad = jnp.zeros((FP - F, T), F32)
    h_copies = []
    for m, v in enumerate((gate_grad, up_grad, hidden)):
        HT[0, m * FP:(m + 1) * FP, :] = jnp.concatenate([v, pad], axis=0).astype(BF16)
        for r in range(1, NX):
            cp = remote(
                HT.at[0, pl.ds(m * FP, FP), :], HT.at[r, pl.ds(m * FP, FP), :],
                h_s.at[m, r - 1], h_r.at[m, r - 1], xnext[r - 1],
            )
            cp.start()
            h_copies.append(cp)
        HR[m] = v.T.astype(BF16)

    def terms(ph):
        rows = rows_of(zhp[ph], 0, ZROWS)

        def step(i, carry):
            cols = pl.ds(pl.multiple_of(i * XC, 128), XC)
            dot = functools.partial(jnp.dot, preferred_element_type=F32)
            TERM[0, rows, cols] = dot(HR[2, rows, :], W[2, :, cols]).astype(BF16)
            TERM[1, rows, cols] = (
                dot(HR[0, rows, :], W[0, :, cols]) + dot(HR[1, rows, :], W[1, :, cols])
            ).astype(BF16)
            return carry

        lax.fori_loop(0, NX, step, 0)
        cp = remote(TERM.at[oc, rows, :], SIB.at[rows, :], ts_s.at[ph], ts_r.at[ph], sibling)
        cp.start()
        started.append(cp)
        return cp

    term_copies = {ph: terms(ph) for ph in (1, 0)}

    def t_copy(a, r, ph, ss, rs):
        ref = TR.at[a, r - 1, rows_of(zhp[ph], 0, ZROWS), :]
        return remote(ref, ref, ss.at[r - 1, ph], rs.at[r - 1, ph], sibling)

    for ph in range(2):
        for r in range(1, NX):
            t_copy(c, r, ph, t_s, t_r).wait_recv()
            cp = t_copy(c, r, ph, tf_s, tf_r)
            cp.start()
            started.append(cp)

    def shares(ph, yv, h):
        rows = rows_of(zhp[ph], yv)
        return TERM[c, rows, half_of(h)].astype(F32) + SIB[rows, half_of(h)].astype(F32)

    def rs_has(dr, k, h):
        return k >= 1 and (k > 1 or h == dr)

    def rs_copy(ph, dr, k, h):
        return remote(
            SB.at[ph, dr, k - 1, h], RB.at[ph, dr, k - 1, h],
            rs_s.at[ph, dr, k - 1, h], rs_r.at[ph, dr, k - 1, h], ynext[dr],
        )

    def rs_send(ph, dr, k, h):
        value = shares(ph, (y + 2 * NY + sgn(dr) * (NK + 1 - k)) % NY, h)
        if rs_has(dr, k - 1, h):
            rs_copy(ph, dr, k - 1, h).wait_recv()
            value = value + RB[ph, dr, k - 2, h].astype(F32)
        SB[ph, dr, k - 1, h] = value.astype(BF16)
        cp = rs_copy(ph, dr, k, h)
        cp.start()
        started.append(cp)

    def rs_open(ph):
        term_copies[ph].wait_recv()
        for dr in range(2):
            rs_send(ph, dr, 1, dr)
        for dr in range(2):
            rs_send(ph, dr, 2, 1 - dr)

    def rs_step(ph, k):
        for h in range(2):
            for dr in range(2):
                if k > 2 or h == dr:
                    rs_send(ph, dr, k, h)

    def rs_total(ph):
        parts = []
        for h in range(2):
            value = shares(ph, y, h)
            for dr in range(2):
                if rs_has(dr, NK, h):
                    rs_copy(ph, dr, NK, h).wait_recv()
                    value = value + RB[ph, dr, NK - 1, h].astype(F32)
            parts.append(value)
        return jnp.concatenate(parts, axis=1)

    rz = remote(ZS, ZR, rz_s, rz_r, zpartner)

    def rs_partner():
        ZS[...] = rs_total(1).astype(BF16)
        rz.start()

    final = remote(xs, xr, fs_s, fs_r, sibling)

    def rs_own():
        total = rs_total(0)
        rz.wait_recv()
        total = total + ZR[...].astype(F32)
        first, second = total[0:8, :], total[8:16, :]
        xs[...] = jnp.where(c == 0, second, first)
        final.start()
        final.wait()
        mine = jnp.where(c == 0, first, second)
        other = xr[...]
        mixed_ref[...] = (combine * jnp.where(c == 0, mine, other)).astype(BF16)
        tgrad_ref[...] = jnp.where(c == 0, other, mine).astype(BF16)

    def weight_part(m):
        a = 0 if m < 2 else 1
        if m == 0:
            for ph in range(2):
                for r in range(1, NX):
                    t_copy(oc, r, ph, tf_s, tf_r).wait_recv()
        total = jnp.dot(
            HT[0, m * FP:(m + 1) * FP, :], G[a, :, pl.ds(pl.multiple_of(x * XC, 128), XC)],
            preferred_element_type=F32,
        )
        for r in range(1, NX):
            h_copies[m * (NX - 1) + r - 1].wait_recv()
            total = total + jnp.dot(
                HT[r, m * FP:(m + 1) * FP, :], TR[a, r - 1], preferred_element_type=F32
            )
        for d in range(NZ):
            DW[m, d] = total[:, d * 128:(d + 1) * 128]

    n = NZ - 1

    def z_copy(dr, m, d):
        return remote(
            SZ.at[dr, m, d], RZ.at[dr, m, d], z_s.at[dr, m, d], z_r.at[dr, m, d], znext[dr]
        )

    def z_sends(dr, d):
        return q < d if dr == 0 else q > d

    def z_gets(dr):
        return q > 0 if dr == 0 else q < NZ - 1

    def z_slot(slot, carry):
        for dr in range(2):
            i = slot - HOP * (q if dr == 0 else NZ - 1 - q)
            m, j = jnp.maximum(i, 0) // n, jnp.maximum(i, 0) % n
            d = NZ - 1 - j if dr == 0 else j

            @pl.when((i >= 0) & (i < 3 * n) & z_sends(dr, d))
            def _():
                @pl.when(z_gets(dr))
                def _():
                    z_copy(dr, m, d).wait_recv()
                value = DW[m, d] + jnp.where(z_gets(dr), RZ[dr, m, d].astype(F32), 0.0)
                SZ[dr, m, d] = value.astype(BF16)
                z_copy(dr, m, d).start()
        return carry

    slots = 3 * n + HOP * n
    marks = {}
    rs_open(1)
    rs_open(0)
    later = [functools.partial(rs_step, ph, k) for k in range(2, NK + 1) for ph in (1, 0)]
    later += [rs_partner]
    for i, f in enumerate(later):
        marks.setdefault(min(2 + 2 * i, slots - 1), []).append(f)
    begin = 0
    for slot in range(slots + 1):
        here = marks.get(slot, [])
        dw = slot % n == 0 and slot // n < 3
        if (here or dw or slot == slots) and slot > begin:
            lax.fori_loop(begin, slot, z_slot, 0)
            begin = slot
        if dw:
            weight_part(slot // n)
        for f in here:
            f()
    rs_own()
    for m in range(3):
        value = DW[m, q]
        for dr in range(2):
            @pl.when(z_gets(dr))
            def _():
                z_copy(dr, m, q).wait_recv()
            value = value + jnp.where(z_gets(dr), RZ[dr, m, q].astype(F32), 0.0)
        wgrad_ref[m] = value[:F, :].astype(BF16)

    for cp in started:
        cp.wait_send()
    for cp in h_copies:
        cp.wait_send()
    az.wait_send()
    rz.wait_send()
    for ph in range(2):
        ref = G.at[c, rows_of(zhp[ph], 0, ZROWS), :]
        remote(ref, ref, sib_s.at[ph], sib_r.at[ph], sibling).wait_send()
        for r in range(1, NX):
            t_copy(c, r, ph, t_s, t_r).wait_send()
    for dr in range(2):
        def drain(i, carry):
            m, d = i // NZ, i % NZ

            @pl.when(z_sends(dr, d))
            def _():
                z_copy(dr, m, d).wait_send()
            return carry
        lax.fori_loop(0, 3 * NZ, drain, 0)


def body(sizes, tokens, row_gate, block_mask, weights, out_grad):
    NX, NZ, NY = sizes
    NK = NY // 2
    D = tokens.shape[1]
    F = weights.shape[1]
    FP = -(-F // 16) * 16
    T = NY * 32
    gate = jnp.broadcast_to(row_gate.astype(F32)[:, None], (8, 128))
    vmem = pl.BlockSpec(memory_space=pltpu.VMEM)
    dma = pltpu.SemaphoreType.DMA
    V = pltpu.VMEM
    return pl.pallas_call(
        functools.partial(kernel, sizes),
        out_shape=(
            jax.ShapeDtypeStruct((8, D), BF16),
            jax.ShapeDtypeStruct((8, D), BF16),
            jax.ShapeDtypeStruct((3, F, 128), BF16),
        ),
        in_specs=[vmem, vmem, vmem, pl.BlockSpec(memory_space=pltpu.SMEM), pl.BlockSpec(memory_space=pl.ANY)],
        out_specs=(vmem, vmem, vmem),
        scratch_shapes=[
            V((8, D), F32), V((8, D), F32),
            V((2, T, D), BF16),
            V((2, NX - 1, T, D // NX), BF16),
            V((3, F, D), BF16),
            V((NX, 3 * FP, T), BF16),
            V((3, T, F), BF16),
            V((2, T, D), BF16), V((T, D), BF16),
            V((2, 2, NK, 2, 16, D // 2), BF16), V((2, 2, NK, 2, 16, D // 2), BF16),
            V((16, D), BF16), V((16, D), BF16),
            V((3, NZ, FP, 128), F32),
            V((2, 3, NZ, FP, 128), BF16), V((2, 3, NZ, FP, 128), BF16),
            dma, dma, dma, dma, dma,
            dma((2, 2, NK, 2)), dma((2, 2, NK, 2)),
            dma((2,)), dma((2,)),
            dma((NX - 1, 2)), dma((NX - 1, 2)),
            dma((NX - 1, 2)), dma((NX - 1, 2)),
            dma((3, NX - 1)), dma((3, NX - 1)),
            dma((2,)), dma((2,)),
            dma((2, 2, NK, 2)), dma((2, 2, NK, 2)),
            dma, dma, dma, dma,
            dma((2, 3, NZ)), dma((2, 3, NZ)),
        ],
        compiler_params=pltpu.CompilerParams(
            collective_id=0, has_side_effects=True, vmem_limit_bytes=48 << 20
        ),
        cost_estimate=pl.CostEstimate(flops=9 * 2 * T * D * F, bytes_accessed=8 * D * F, transcendentals=T * F),
    )(tokens, out_grad, gate, block_mask, weights)


def solution(mesh):
    in_specs = (
        P(("dp", "expert"), None),
        P(("dp", "expert")),
        P("dp"),
        P(None, "expert", None),
        P(("dp", "expert"), None),
    )
    out_specs = (P(("dp", "expert"), None), P(("dp", "expert"), None), P(None, "expert", "dp"))
    return jax.shard_map(
        functools.partial(body, SIZES), mesh=mesh, in_specs=in_specs, out_specs=out_specs, check_vma=False
    )
```

time: 693 us -> 102 us (0.15)
  the two profiles are of different devices: /device:TPU:1 before, /device:TPU:2 now
where the time goes in v1:
time: 102 us
  Pallas kernels  94.2 us (92%)
  local copies, waits for them, and re-layouts  6.74 us (7%)
    pallas_call x1, Pallas kernels, body(): pl.pallas_call(functools.partial(kernel, sizes), out_shape=(jax.ShapeDtyp...  94.2 us
    unnamed x11, local copies, waits for them, and re-layouts  6.02 us

profile of v1, /device:TPU:2, one launch (start us, length us, event | category | flops | bytes accessed | tf_op | source)
XLA Modules:
  0.0 101.6 jit_solution(16253600928098859220)
XLA Ops:
  0.6 0.7 broadcast_in_dim.2.gate_ref
  1.4 0.0 copy-start
  1.4 1.9 %copy-done = bf16[3,168,3072]{2,1,0:T(8,128)(2,1)S(1)} copy-done((bf16[3,168,3072]{2,1,0:T(8,128)(2,1)S(1)}, bf16[3,168,3072]{2,1,0:T(8,128)(2,1)}, u32[]{:S(2)}) %copy-start) | copy-done | bytes 3096600
  3.2 0.0 copy-start.1
  3.2 0.8 copy-done.1
  4.0 0.0 copy-start.2
  4.0 0.8 copy-done.2
  4.8 0.0 copy-start.3
  4.8 0.7 copy-done.3
  5.5 94.2 %shard_map.76 = (bf16[8,3072]{1,0:T(8,128)(2,1)S(1)}, bf16[8,3072]{1,0:T(8,128)(2,1)S(1)}, bf16[3,168,128]{2,1,0:T(8,128)(2,1)S(1)}) custom-call(bf16[8,3072]{1,0:T(8,128)(2,1)S(1)} %copy-done.1, bf16[8,3072]{1,0:T(8,128)(2,1)S(1)} %copy-done.2, f32[8,128]{1,0:T(8,128)S(1)} %broadcast_in_dim.2.gate_ref, s32[2]{0:T(128)S(1)} %copy-done.3, ...), custom_call_target="tpu_custom_call" | custom-call | flops 2378170368 | bytes 4128768 | tf_op jit(solution)/shard_map/pallas_call | solution.py:393
  99.7 0.6 copy.11
  100.4 0.6 copy.12
  101.0 0.7 copy.13
Async XLA Ops:
  1.4 1.9 %copy-start = (bf16[3,168,3072]{2,1,0:T(8,128)(2,1)S(1)}, bf16[3,168,3072]{2,1,0:T(8,128)(2,1)}, u32[]{:S(2)}) copy-start(bf16[3,168,3072]{2,1,0:T(8,128)(2,1)} %w_hbm.1) | copy-start | bytes 9289732
  3.2 0.8 copy-start.1
  4.0 0.8 copy-start.2
  4.8 0.7 copy-start.3

commit v2 on v1

--- a/solution.py
+++ b/solution.py
@@ -12,7 +12,9 @@
 BF16 = jnp.bfloat16
 
 SIZES = (4, 6, 8)
-HOP = 2
+HOP = 3
+FIRST = (0, 2, 4)
+EARLY = True
 
 
 def kernel(
@@ -112,6 +114,8 @@
 
     def ag_first(ph):
         for h in range(2):
+            if ph == 1:
+                az_copy(rows_of(oz, y), h).wait_recv()
             for dr in range(2):
                 if ag_has(dr, 1, h):
                     ag_send(ph, dr, 1, h)
@@ -130,57 +134,78 @@
         if k < NK:
             spread(ph, (y + k) % NY)
 
-    az = remote(G.at[c, my_rows, :], G.at[c, my_rows, :], az_s, az_r, zpartner)
-    az.start()
+    def az_copy(rows, h):
+        ref = G.at[c, rows, half_of(h)]
+        return remote(ref, ref, az_s.at[h], az_r.at[h], zpartner)
+
+    for h in range(2):
+        cp = az_copy(my_rows, h)
+        cp.start()
+        started.append(cp)
+
+    def contract(m, a, ph):
+        rows = rows_of(zhp[ph], 0, ZROWS)
+
+        def step(i, acc):
+            cols = pl.ds(pl.multiple_of(i * XC, 128), XC)
+            return acc + lax.dot_general(
+                W[m, :, cols], G[a, rows, cols], (((1,), (1,)), ((), ())), preferred_element_type=F32
+            )
+        return lax.fori_loop(0, NX, step, jnp.zeros((F, ZROWS), F32))
+
+    def h_copy(ph, m, r):
+        spot = (pl.ds(m * FP, FP), pl.ds(pl.multiple_of(zhp[ph] * ZROWS, ZROWS), ZROWS))
+        return remote(
+            HT.at[0, *spot], HT.at[r, *spot], h_s.at[ph, m, r - 1], h_r.at[ph, m, r - 1], xnext[r - 1]
+        )
+
+    held = {}
+
+    def hidden_first(ph):
+        ref = G.at[oc, rows_of(zhp[ph], 0, ZROWS), :]
+        remote(ref, ref, sib_s.at[ph], sib_r.at[ph], sibling).wait_recv()
+        if ph == 0:
+            w_copy.wait()
+        held[ph] = contract(0, 0, ph), contract(1, 0, ph)
+
+    def hidden_second(ph):
+        pre_gate, pre_up = held[ph]
+        back = contract(2, 1, ph)
+        live = mask_ref[zhp[ph]].astype(F32)
+        sig = jax.nn.sigmoid(pre_gate)
+        silu = pre_gate * sig
+        hidden = live * silu * pre_up
+        gate_grad = live * back * pre_up * (sig * (1.0 + pre_gate * (1.0 - sig)))
+        up_grad = live * back * silu
+        pad = jnp.zeros((FP - F, ZROWS), F32)
+        lanes = pl.ds(pl.multiple_of(zhp[ph] * ZROWS, ZROWS), ZROWS)
+        for m, v in enumerate((gate_grad, up_grad, hidden)):
+            HT[0, m * FP:(m + 1) * FP, lanes] = jnp.concatenate([v, pad], axis=0).astype(BF16)
+            for r in range(1, NX):
+                h_copy(ph, m, r).start()
+        for m, v in enumerate((gate_grad, up_grad, hidden)):
+            HR[m, rows_of(zhp[ph], 0, ZROWS), :] = v.T.astype(BF16)
+
     ag_first(0)
-    order = [(0, k) for k in range(1, NK // 2 + 1)] + [(1, 0)]
     late0 = [(0, k) for k in range(NK // 2 + 1, NK + 1)]
     late1 = [(1, k) for k in range(1, NK + 1)]
+    order = [(0, k) for k in range(1, NK // 2 + 1)] + [(1, 0)]
     while late0 or late1:
         if late0:
             order.append(late0.pop(0))
         if late1:
             order.append(late1.pop(0))
+    work = [functools.partial(hidden_first, 0), functools.partial(hidden_second, 0)]
     for ph, k in order:
         if k == 0:
-            there = G.at[c, rows_of(oz, y), :]
-            remote(there, there, az_s, az_r, zpartner).wait_recv()
             ag_first(1)
         else:
             ag_step(ph, k)
-    w_copy.wait()
-    for ph in range(2):
-        ref = G.at[oc, rows_of(zhp[ph], 0, ZROWS), :]
-        remote(ref, ref, sib_s.at[ph], sib_r.at[ph], sibling).wait_recv()
-
-    def contract(m, a):
-        def step(i, acc):
-            cols = pl.ds(pl.multiple_of(i * XC, 128), XC)
-            return acc + lax.dot_general(
-                W[m, :, cols], G[a, :, cols], (((1,), (1,)), ((), ())), preferred_element_type=F32
-            )
-        return lax.fori_loop(0, NX, step, jnp.zeros((F, T), F32))
-
-    pre_gate, pre_up, back = contract(0, 0), contract(1, 0), contract(2, 1)
-    lane = lax.broadcasted_iota(jnp.int32, (1, T), 1)
-    live = jnp.where(lane < T // 2, mask_ref[0], mask_ref[1]).astype(F32)
-    sig = jax.nn.sigmoid(pre_gate)
-    silu = pre_gate * sig
-    hidden = live * silu * pre_up
-    gate_grad = live * back * pre_up * (sig * (1.0 + pre_gate * (1.0 - sig)))
-    up_grad = live * back * silu
-    pad = jnp.zeros((FP - F, T), F32)
-    h_copies = []
-    for m, v in enumerate((gate_grad, up_grad, hidden)):
-        HT[0, m * FP:(m + 1) * FP, :] = jnp.concatenate([v, pad], axis=0).astype(BF16)
-        for r in range(1, NX):
-            cp = remote(
-                HT.at[0, pl.ds(m * FP, FP), :], HT.at[r, pl.ds(m * FP, FP), :],
-                h_s.at[m, r - 1], h_r.at[m, r - 1], xnext[r - 1],
-            )
-            cp.start()
-            h_copies.append(cp)
-        HR[m] = v.T.astype(BF16)
+        if EARLY and ph == 1 and k >= NK - 2 and work:
+            work.pop(0)()
+    work += [functools.partial(hidden_first, 1), functools.partial(hidden_second, 1)]
+    for f in work:
+        f()
 
     def terms(ph):
         rows = rows_of(zhp[ph], 0, ZROWS)
@@ -292,7 +317,8 @@
             preferred_element_type=F32,
         )
         for r in range(1, NX):
-            h_copies[m * (NX - 1) + r - 1].wait_recv()
+            for ph in range(2):
+                h_copy(ph, m, r).wait_recv()
             total = total + jnp.dot(
                 HT[r, m * FP:(m + 1) * FP, :], TR[a, r - 1], preferred_element_type=F32
             )
@@ -312,10 +338,27 @@
     def z_gets(dr):
         return q > 0 if dr == 0 else q < NZ - 1
 
+    left = {m: 0 for m in range(3)}
+    stream = []
+    for i in range(3 * n):
+        ready = [m for m in range(3) if left[m] < n and (FIRST[m] <= i or m == 0)]
+        ready = ready or [m for m in range(3) if left[m] < n]
+        m = min(ready, key=lambda m: (left[m], m))
+        stream.append((m, left[m]))
+        left[m] += 1
+    first_use = [min(i for i, v in enumerate(stream) if v[0] == m) for m in range(3)]
+
+    def looked_up(i, which):
+        value = jnp.int32(0)
+        for k, v in enumerate(stream):
+            if v[which]:
+                value = jnp.where(i == k, v[which], value)
+        return value
+
     def z_slot(slot, carry):
         for dr in range(2):
             i = slot - HOP * (q if dr == 0 else NZ - 1 - q)
-            m, j = jnp.maximum(i, 0) // n, jnp.maximum(i, 0) % n
+            m, j = looked_up(i, 0), looked_up(i, 1)
             d = NZ - 1 - j if dr == 0 else j
 
             @pl.when((i >= 0) & (i < 3 * n) & z_sends(dr, d))
@@ -339,12 +382,12 @@
     begin = 0
     for slot in range(slots + 1):
         here = marks.get(slot, [])
-        dw = slot % n == 0 and slot // n < 3
+        dw = slot in first_use
         if (here or dw or slot == slots) and slot > begin:
             lax.fori_loop(begin, slot, z_slot, 0)
             begin = slot
         if dw:
-            weight_part(slot // n)
+            weight_part(first_use.index(slot))
         for f in here:
             f()
     rs_own()
@@ -359,9 +402,10 @@
 
     for cp in started:
         cp.wait_send()
-    for cp in h_copies:
-        cp.wait_send()
-    az.wait_send()
+    for ph in range(2):
+        for m in range(3):
+            for r in range(1, NX):
+                h_copy(ph, m, r).wait_send()
     rz.wait_send()
     for ph in range(2):
         ref = G.at[c, rows_of(zhp[ph], 0, ZROWS), :]
@@ -411,19 +455,19 @@
             V((16, D), BF16), V((16, D), BF16),
             V((3, NZ, FP, 128), F32),
             V((2, 3, NZ, FP, 128), BF16), V((2, 3, NZ, FP, 128), BF16),
-            dma, dma, dma, dma, dma,
+            dma, dma, dma, dma((2,)), dma((2,)),
             dma((2, 2, NK, 2)), dma((2, 2, NK, 2)),
             dma((2,)), dma((2,)),
             dma((NX - 1, 2)), dma((NX - 1, 2)),
             dma((NX - 1, 2)), dma((NX - 1, 2)),
-            dma((3, NX - 1)), dma((3, NX - 1)),
+            dma((2, 3, NX - 1)), dma((2, 3, NX - 1)),
             dma((2,)), dma((2,)),
             dma((2, 2, NK, 2)), dma((2, 2, NK, 2)),
             dma, dma, dma, dma,
             dma((2, 3, NZ)), dma((2, 3, NZ)),
         ],
         compiler_params=pltpu.CompilerParams(
-            collective_id=0, has_side_effects=True, vmem_limit_bytes=48 << 20
+            collective_id=0, has_side_effects=True, vmem_limit_bytes=60 << 20
         ),
         cost_estimate=pl.CostEstimate(flops=9 * 2 * T * D * F, bytes_accessed=8 * D * F, transcendentals=T * F),
     )(tokens, out_grad, gate, block_mask, weights)

time: 102 us -> 93.6 us (0.918)
  the two profiles are of different devices: /device:TPU:2 before, /device:TPU:1 now
where the time goes in v2:
time: 93.6 us; the launch traced here: 93.2 us
  Pallas kernels  86.9 us (93%)
  local copies, waits for them, and re-layouts  5.72 us (6%)
    pallas_call x1, Pallas kernels, body(): pl.pallas_call(functools.partial(kernel, sizes), out_shape=(jax.ShapeDtyp...  86.9 us
    unnamed x3, local copies, waits for them, and re-layouts  4.4 us

profile of v2, /device:TPU:1, one launch (start us, length us, event | category | flops | bytes accessed | tf_op | source)
XLA Modules:
  0.0 93.2 jit_solution(8773438623049768061)
XLA Ops:
  0.6 1.3 %broadcast_in_dim.2.gate_ref = f32[8,128]{1,0:T(8,128)} broadcast(bf16[8]{0:T(256)(128)(2,1)} %param.6), dimensions={0} | broadcast | bytes 4112 | tf_op jit(solution)/shard_map/broadcast_in_dim | solution.py:433
  1.9 86.9 %shard_map.76 = (bf16[8,3072]{1,0:T(8,128)(2,1)}, bf16[8,3072]{1,0:T(8,128)(2,1)}, bf16[3,168,128]{2,1,0:T(8,128)(2,1)}) custom-call(bf16[8,3072]{1,0:T(8,128)(2,1)} %tok_ref.1, bf16[8,3072]{1,0:T(8,128)(2,1)} %og_ref.1, f32[8,128]{1,0:T(8,128)} %broadcast_in_dim.2.gate_ref, s32[2]{0:T(128)} %mask_ref.1, bf16[3,168,3072]{2,1,0:T(8,128)(2,1)} %w_hbm.1), custom_call_target="tpu_custom_call" | custom-call | flops 2378170368 | bytes 4128768 | tf_op jit(solution)/shard_map/pallas_call | solution.py:437
  88.8 1.4 %copy.11 = bf16[8,3072]{1,0:T(8,128)(2,1)} copy(bf16[8,3072]{1,0:T(8,128)(2,1)} %get-tuple-element.6) | data formatting | bytes 98304
  90.2 1.4 %copy.12 = bf16[8,3072]{1,0:T(8,128)(2,1)} copy(bf16[8,3072]{1,0:T(8,128)(2,1)} %get-tuple-element.7) | data formatting | bytes 98304
  91.7 1.6 %copy.13 = bf16[3,168,128]{2,1,0:T(8,128)(2,1)} copy(bf16[3,168,128]{2,1,0:T(8,128)(2,1)} %get-tuple-element.8) | data formatting | bytes 258048

commit v3 on v2

--- a/solution.py
+++ b/solution.py
@@ -15,17 +15,18 @@
 HOP = 3
 FIRST = (0, 2, 4)
 EARLY = True
+STEPS = (1, 2, 3)
 
 
 def kernel(
-    sizes, tok_ref, og_ref, gate_ref, mask_ref, w_hbm, mixed_ref, tgrad_ref, wgrad_ref,
+    sizes, tok_hbm, og_hbm, gate_ref, mask_ref, w_hbm, rows_ref, wgrad_ref,
     xs, xr, G, TR, W, HT, HR, TERM, SIB, SB, RB, ZS, ZR, DW, SZ, RZ,
-    w_sem, xs_s, xs_r, az_s, az_r, ag_s, ag_r, sib_s, sib_r, t_s, t_r, tf_s, tf_r,
+    in_v, in_sem, w_sem, xs_s, xs_r, az_s, az_r, ag_s, ag_r, sib_s, sib_r, t_s, t_r, tf_s, tf_r,
     h_s, h_r, ts_s, ts_r, rs_s, rs_r, rz_s, rz_r, fs_s, fs_r, z_s, z_r,
 ):
     NX, NZ, NY = sizes
     NK = NY // 2
-    D = tok_ref.shape[1]
+    D = tok_hbm.shape[1]
     F = W.shape[1]
     FP = HT.shape[1] // 3
     T = G.shape[1]
@@ -55,6 +56,9 @@
     znext = (at(q=(q + 1) % NZ), at(q=(q + NZ - 1) % NZ))
 
     w_copy = pltpu.make_async_copy(w_hbm, W, w_sem)
+    loads = [pltpu.make_async_copy(r, in_v.at[i], in_sem.at[i]) for i, r in enumerate((tok_hbm, og_hbm))]
+    for cp in loads:
+        cp.start()
     w_copy.start()
 
     barrier = pltpu.get_barrier_semaphore()
@@ -62,9 +66,13 @@
     for p in partners:
         pl.semaphore_signal(barrier, inc=1, device_id=p, device_id_type=MESH)
 
-    tok = tok_ref[...].astype(F32)
-    combine = gate_ref[:, 0:1]
-    rg = (combine * og_ref[...].astype(F32)).astype(BF16).astype(F32)
+    for cp in loads:
+        cp.wait()
+    tok = in_v[0].astype(F32)
+    spot = (lax.broadcasted_iota(jnp.int32, (8, 8), 0), lax.broadcasted_iota(jnp.int32, (8, 8), 1))
+    gates = jnp.broadcast_to(gate_ref[...].astype(F32), (8, 8))
+    combine = jnp.sum(jnp.where(spot[0] == spot[1], gates, 0.0), axis=1, keepdims=True)
+    rg = (combine * in_v[1].astype(F32)).astype(BF16).astype(F32)
     xs[...] = jnp.where(c == 0, rg, tok)
     pl.semaphore_wait(barrier, len(partners))
 
@@ -75,76 +83,96 @@
     own = jnp.where(c == 0, tok, rg)
     block = jnp.concatenate([jnp.where(c == 0, own, got), jnp.where(c == 0, got, own)], axis=0)
 
-    def rows_of(zhv, yv, n=16):
-        return pl.ds(pl.multiple_of((zhv * NY + yv) * 16, 16), n)
+    def place(o):
+        return 0 if o == 0 else (2 * NK - 1 if abs(o) == NK else 2 * abs(o) - (o < 0))
+
+    def rows_at(ph, first, n=1):
+        return pl.ds(ph * ZROWS + first * 16, n * 16)
+
+    def rows_of(ph, o):
+        return rows_at(ph, place(o))
+
+    def rows_all(ph):
+        return pl.ds(ph * ZROWS, ZROWS)
 
     def half_of(h):
         return pl.ds(h * HALF, HALF)
 
-    my_rows = rows_of(zh, y)
-    G[c, my_rows, :] = block.astype(BF16)
+    G[c, 0:16, :] = block.astype(BF16)
 
     def sgn(dr):
         return 1 if dr == 0 else -1
 
-    def ag_copy(ph, dr, k, h, origin):
-        ref = G.at[c, rows_of(zhp[ph], origin), half_of(h)]
-        return remote(ref, ref, ag_s.at[ph, dr, k - 1, h], ag_r.at[ph, dr, k - 1, h], ynext[dr])
+    def ag_copy(ph, dr, k, h):
+        o = -sgn(dr)
+        return remote(
+            G.at[c, rows_of(ph, o * (k - 1)), half_of(h)], G.at[c, rows_of(ph, o * k), half_of(h)],
+            ag_s.at[ph, dr, k - 1, h], ag_r.at[ph, dr, k - 1, h], ynext[dr],
+        )
 
     started = []
 
     def ag_send(ph, dr, k, h):
-        cp = ag_copy(ph, dr, k, h, (y + 2 * NY - sgn(dr) * (k - 1)) % NY)
+        cp = ag_copy(ph, dr, k, h)
         cp.start()
         started.append(cp)
 
-    def spread(ph, origin):
-        rows = rows_of(zhp[ph], origin)
+    def spread(ph, first, n):
+        rows = rows_at(ph, first, n)
         ref = G.at[c, rows, :]
         remote(ref, ref, sib_s.at[ph], sib_r.at[ph], sibling).start()
         for r in range(1, NX):
-            cols = pl.ds(pl.multiple_of(((x + r) % NX) * XC, 128), XC)
             remote(
-                G.at[c, rows, cols], TR.at[c, r - 1, rows, :],
+                G.at[c, rows, xcols[r]], TR.at[c, r - 1, rows, :],
                 t_s.at[r - 1, ph], t_r.at[r - 1, ph], xnext[r - 1],
             ).start()
 
+    xcols = [pl.ds(pl.multiple_of(((x + r) % NX) * XC, 128), XC) for r in range(NX)]
+
     def ag_has(dr, k, h):
         return k < NK or h == dr
+
+    def az_copy(h):
+        return remote(
+            G.at[c, rows_of(0, 0), half_of(h)], G.at[c, rows_of(1, 0), half_of(h)], az_s.at[h], az_r.at[h], zpartner
+        )
 
     def ag_first(ph):
         for h in range(2):
             if ph == 1:
-                az_copy(rows_of(oz, y), h).wait_recv()
+                az_copy(h).wait_recv()
             for dr in range(2):
                 if ag_has(dr, 1, h):
                     ag_send(ph, dr, 1, h)
-        spread(ph, y)
 
     def ag_step(ph, k):
         for h in range(2):
             for dr in range(2):
                 if not ag_has(dr, k, h):
                     continue
-                origin = (y + 2 * NY - sgn(dr) * k) % NY
-                ag_copy(ph, dr, k, h, origin).wait_recv()
+                ag_copy(ph, dr, k, h).wait_recv()
                 if k < NK and ag_has(dr, k + 1, h):
                     ag_send(ph, dr, k + 1, h)
-        spread(ph, (y + NY - k) % NY)
-        if k < NK:
-            spread(ph, (y + k) % NY)
-
-    def az_copy(rows, h):
-        ref = G.at[c, rows, half_of(h)]
-        return remote(ref, ref, az_s.at[h], az_r.at[h], zpartner)
+        if (ph, k) in BATCH:
+            first, n = BATCH[ph, k]
+            spread(ph, first, n)
+
+    BATCH = {}
+    for ph in range(2):
+        begin = 0
+        for k in STEPS:
+            if k < NK:
+                BATCH[ph, k] = (begin, 2 * k + 1 - begin)
+                begin = 2 * k + 1
+        BATCH[ph, NK] = (begin, 2 * NK - begin)
 
     for h in range(2):
-        cp = az_copy(my_rows, h)
+        cp = az_copy(h)
         cp.start()
         started.append(cp)
 
     def contract(m, a, ph):
-        rows = rows_of(zhp[ph], 0, ZROWS)
+        rows = rows_all(ph)
 
         def step(i, acc):
             cols = pl.ds(pl.multiple_of(i * XC, 128), XC)
@@ -154,7 +182,7 @@
         return lax.fori_loop(0, NX, step, jnp.zeros((F, ZROWS), F32))
 
     def h_copy(ph, m, r):
-        spot = (pl.ds(m * FP, FP), pl.ds(pl.multiple_of(zhp[ph] * ZROWS, ZROWS), ZROWS))
+        spot = (pl.ds(m * FP, FP), rows_all(ph))
         return remote(
             HT.at[0, *spot], HT.at[r, *spot], h_s.at[ph, m, r - 1], h_r.at[ph, m, r - 1], xnext[r - 1]
         )
@@ -162,7 +190,7 @@
     held = {}
 
     def hidden_first(ph):
-        ref = G.at[oc, rows_of(zhp[ph], 0, ZROWS), :]
+        ref = G.at[oc, rows_all(ph), :]
         remote(ref, ref, sib_s.at[ph], sib_r.at[ph], sibling).wait_recv()
         if ph == 0:
             w_copy.wait()
@@ -178,13 +206,13 @@
         gate_grad = live * back * pre_up * (sig * (1.0 + pre_gate * (1.0 - sig)))
         up_grad = live * back * silu
         pad = jnp.zeros((FP - F, ZROWS), F32)
-        lanes = pl.ds(pl.multiple_of(zhp[ph] * ZROWS, ZROWS), ZROWS)
+        lanes = rows_all(ph)
         for m, v in enumerate((gate_grad, up_grad, hidden)):
             HT[0, m * FP:(m + 1) * FP, lanes] = jnp.concatenate([v, pad], axis=0).astype(BF16)
             for r in range(1, NX):
                 h_copy(ph, m, r).start()
         for m, v in enumerate((gate_grad, up_grad, hidden)):
-            HR[m, rows_of(zhp[ph], 0, ZROWS), :] = v.T.astype(BF16)
+            HR[m, rows_all(ph), :] = v.T.astype(BF16)
 
     ag_first(0)
     late0 = [(0, k) for k in range(NK // 2 + 1, NK + 1)]
@@ -208,7 +236,7 @@
         f()
 
     def terms(ph):
-        rows = rows_of(zhp[ph], 0, ZROWS)
+        rows = rows_all(ph)
 
         def step(i, carry):
             cols = pl.ds(pl.multiple_of(i * XC, 128), XC)
@@ -228,7 +256,7 @@
     term_copies = {ph: terms(ph) for ph in (1, 0)}
 
     def t_copy(a, r, ph, ss, rs):
-        ref = TR.at[a, r - 1, rows_of(zhp[ph], 0, ZROWS), :]
+        ref = TR.at[a, r - 1, rows_all(ph), :]
         return remote(ref, ref, ss.at[r - 1, ph], rs.at[r - 1, ph], sibling)
 
     for ph in range(2):
@@ -238,8 +266,8 @@
             cp.start()
             started.append(cp)
 
-    def shares(ph, yv, h):
-        rows = rows_of(zhp[ph], yv)
+    def shares(ph, o, h):
+        rows = rows_of(ph, o)
         return TERM[c, rows, half_of(h)].astype(F32) + SIB[rows, half_of(h)].astype(F32)
 
     def rs_has(dr, k, h):
@@ -252,7 +280,7 @@
         )
 
     def rs_send(ph, dr, k, h):
-        value = shares(ph, (y + 2 * NY + sgn(dr) * (NK + 1 - k)) % NY, h)
+        value = shares(ph, sgn(dr) * (NK + 1 - k), h)
         if rs_has(dr, k - 1, h):
             rs_copy(ph, dr, k - 1, h).wait_recv()
             value = value + RB[ph, dr, k - 2, h].astype(F32)
@@ -277,7 +305,7 @@
     def rs_total(ph):
         parts = []
         for h in range(2):
-            value = shares(ph, y, h)
+            value = shares(ph, 0, h)
             for dr in range(2):
                 if rs_has(dr, NK, h):
                     rs_copy(ph, dr, NK, h).wait_recv()
@@ -303,8 +331,8 @@
         final.wait()
         mine = jnp.where(c == 0, first, second)
         other = xr[...]
-        mixed_ref[...] = (combine * jnp.where(c == 0, mine, other)).astype(BF16)
-        tgrad_ref[...] = jnp.where(c == 0, other, mine).astype(BF16)
+        rows_ref[0] = (combine * jnp.where(c == 0, mine, other)).astype(BF16)
+        rows_ref[1] = jnp.where(c == 0, other, mine).astype(BF16)
 
     def weight_part(m):
         a = 0 if m < 2 else 1
@@ -313,7 +341,7 @@
                 for r in range(1, NX):
                     t_copy(oc, r, ph, tf_s, tf_r).wait_recv()
         total = jnp.dot(
-            HT[0, m * FP:(m + 1) * FP, :], G[a, :, pl.ds(pl.multiple_of(x * XC, 128), XC)],
+            HT[0, m * FP:(m + 1) * FP, :], G[a, :, xcols[0]],
             preferred_element_type=F32,
         )
         for r in range(1, NX):
@@ -378,7 +406,7 @@
     later = [functools.partial(rs_step, ph, k) for k in range(2, NK + 1) for ph in (1, 0)]
     later += [rs_partner]
     for i, f in enumerate(later):
-        marks.setdefault(min(2 + 2 * i, slots - 1), []).append(f)
+        marks.setdefault(min(1 + 2 * i, slots - 1), []).append(f)
     begin = 0
     for slot in range(slots + 1):
         here = marks.get(slot, [])
@@ -408,7 +436,7 @@
                 h_copy(ph, m, r).wait_send()
     rz.wait_send()
     for ph in range(2):
-        ref = G.at[c, rows_of(zhp[ph], 0, ZROWS), :]
+        ref = G.at[c, rows_all(ph), :]
         remote(ref, ref, sib_s.at[ph], sib_r.at[ph], sibling).wait_send()
         for r in range(1, NX):
             t_copy(c, r, ph, t_s, t_r).wait_send()
@@ -430,19 +458,19 @@
     F = weights.shape[1]
     FP = -(-F // 16) * 16
     T = NY * 32
-    gate = jnp.broadcast_to(row_gate.astype(F32)[:, None], (8, 128))
+    gate = row_gate.reshape(1, 8)
     vmem = pl.BlockSpec(memory_space=pltpu.VMEM)
+    hbm = pl.BlockSpec(memory_space=pltpu.HBM)
     dma = pltpu.SemaphoreType.DMA
     V = pltpu.VMEM
-    return pl.pallas_call(
+    rows, weight_grad = pl.pallas_call(
         functools.partial(kernel, sizes),
         out_shape=(
-            jax.ShapeDtypeStruct((8, D), BF16),
-            jax.ShapeDtypeStruct((8, D), BF16),
+            jax.ShapeDtypeStruct((2, 8, D), BF16),
             jax.ShapeDtypeStruct((3, F, 128), BF16),
         ),
-        in_specs=[vmem, vmem, vmem, pl.BlockSpec(memory_space=pltpu.SMEM), pl.BlockSpec(memory_space=pl.ANY)],
-        out_specs=(vmem, vmem, vmem),
+        in_specs=[hbm, hbm, vmem, pl.BlockSpec(memory_space=pltpu.SMEM), hbm],
+        out_specs=(vmem, vmem),
         scratch_shapes=[
             V((8, D), F32), V((8, D), F32),
             V((2, T, D), BF16),
@@ -455,6 +483,7 @@
             V((16, D), BF16), V((16, D), BF16),
             V((3, NZ, FP, 128), F32),
             V((2, 3, NZ, FP, 128), BF16), V((2, 3, NZ, FP, 128), BF16),
+            V((2, 8, D), BF16), dma((2,)),
             dma, dma, dma, dma((2,)), dma((2,)),
             dma((2, 2, NK, 2)), dma((2, 2, NK, 2)),
             dma((2,)), dma((2,)),
@@ -471,6 +500,7 @@
         ),
         cost_estimate=pl.CostEstimate(flops=9 * 2 * T * D * F, bytes_accessed=8 * D * F, transcendentals=T * F),
     )(tokens, out_grad, gate, block_mask, weights)
+    return rows[0], rows[1], weight_grad
 
 
 def solution(mesh):

time: 93.6 us -> 89.8 us (0.959)
  local copies, waits for them, and re-layouts: 5.72 us -> 3.03 us
  Pallas kernels: 86.9 us -> 85.9 us
    unnamed x3 -> x1, local copies, waits for them, and re-layouts: 4.4 us -> 1.56 us
    squeeze x0 -> x1, local copies, waits for them, and re-layouts: none -> 1.46 us  [body(): return (rows[0], rows[1], weight_grad)]
    broadcast_in_dim x1 -> x0, local copies, waits for them, and re-layouts: 1.32 us -> none  [body(): gate = jnp.broadcast_to(row_gate.astype(F32)[:, None], (8, 128))]
    pallas_call x1, Pallas kernels: 86.9 us -> 85.9 us  [body(): pl.pallas_call(functools.partial(kernel, sizes), out_shape=(jax.ShapeDtyp...]
where the time goes in v3:
time: 89.8 us; the launch traced here: 89.6 us
  Pallas kernels  85.9 us (96%)
  local copies, waits for them, and re-layouts  3.03 us (3%)
    pallas_call x1, Pallas kernels, body(): pl.pallas_call(functools.partial(kernel, sizes), out_shape=(jax.ShapeDtyp...  85.9 us

profile of v3, /device:TPU:1, one launch (start us, length us, event | category | flops | bytes accessed | tf_op | source)
XLA Modules:
  0.0 89.6 jit_solution(18233243743843678456)
XLA Ops:
  0.6 85.9 %shard_map.76 = (bf16[2,8,3072]{2,1,0:T(8,128)(2,1)}, bf16[3,168,128]{2,1,0:T(8,128)(2,1)}) custom-call(bf16[8,3072]{1,0:T(8,128)(2,1)} %tok_hbm.1, bf16[8,3072]{1,0:T(8,128)(2,1)} %og_hbm.1, bf16[1,8]{1,0:T(2,128)(2,1)} %bitcast.5, s32[2]{0:T(128)} %mask_ref.1, bf16[3,168,3072]{2,1,0:T(8,128)(2,1)} %w_hbm.1), custom_call_target="tpu_custom_call" | custom-call | flops 2378170368 | bytes 4128768 | tf_op jit(solution)/shard_map/pallas_call | solution.py:466
  86.6 1.5 %slice_bitcast_fusion = (bf16[8,3072]{1,0:T(8,128)(2,1)}, bf16[8,3072]{1,0:T(8,128)(2,1)}) fusion(bf16[2,8,3072]{2,1,0:T(8,128)(2,1)} %get-tuple-element.5), kind=kLoop, calls=%fused_computation | loop fusion | bytes 196608 | tf_op jit(solution)/shard_map/squeeze | solution.py:503
  88.0 1.6 %copy.9 = bf16[3,168,128]{2,1,0:T(8,128)(2,1)} copy(bf16[3,168,128]{2,1,0:T(8,128)(2,1)} %get-tuple-element.14) | data formatting | bytes 258048

commit v4 on v3

--- a/solution.py
+++ b/solution.py
@@ -406,7 +406,7 @@
     later = [functools.partial(rs_step, ph, k) for k in range(2, NK + 1) for ph in (1, 0)]
     later += [rs_partner]
     for i, f in enumerate(later):
-        marks.setdefault(min(1 + 2 * i, slots - 1), []).append(f)
+        marks.setdefault(min(2 * i, slots - 1), []).append(f)
     begin = 0
     for slot in range(slots + 1):
         here = marks.get(slot, [])

time: 89.8 us -> 90.4 us (level)
  no operation moved by 1% of the time
where the time goes in v4:
time: 90.4 us; the launch traced here: 90.2 us
  Pallas kernels  86.5 us (96%)
  local copies, waits for them, and re-layouts  3.03 us (3%)
    pallas_call x1, Pallas kernels, body(): pl.pallas_call(functools.partial(kernel, sizes), out_shape=(jax.ShapeDtyp...  86.5 us

profile of v4, /device:TPU:1, one launch (start us, length us, event | category | flops | bytes accessed | tf_op | source)
XLA Modules:
  0.0 90.2 jit_solution(17374578232272407828)
XLA Ops:
  0.6 86.5 %shard_map.76 = (bf16[2,8,3072]{2,1,0:T(8,128)(2,1)}, bf16[3,168,128]{2,1,0:T(8,128)(2,1)}) custom-call(bf16[8,3072]{1,0:T(8,128)(2,1)} %tok_hbm.1, bf16[8,3072]{1,0:T(8,128)(2,1)} %og_hbm.1, bf16[1,8]{1,0:T(2,128)(2,1)} %bitcast.5, s32[2]{0:T(128)} %mask_ref.1, bf16[3,168,3072]{2,1,0:T(8,128)(2,1)} %w_hbm.1), custom_call_target="tpu_custom_call" | custom-call | flops 2378170368 | bytes 4128768 | tf_op jit(solution)/shard_map/pallas_call | solution.py:466
  87.1 1.5 %slice_bitcast_fusion = (bf16[8,3072]{1,0:T(8,128)(2,1)}, bf16[8,3072]{1,0:T(8,128)(2,1)}) fusion(bf16[2,8,3072]{2,1,0:T(8,128)(2,1)} %get-tuple-element.5), kind=kLoop, calls=%fused_computation | loop fusion | bytes 196608 | tf_op jit(solution)/shard_map/squeeze | solution.py:503
  88.6 1.6 %copy.9 = bf16[3,168,128]{2,1,0:T(8,128)(2,1)} copy(bf16[3,168,128]{2,1,0:T(8,128)(2,1)} %get-tuple-element.14) | data formatting | bytes 258048
